TPU v7x, 32 devices: a whole 2x2x4 slice. The times are simulated.
32 devices in a mesh: row: 4 (over y, x), blk: 8 (over z, core).
Axes of the slice: x: 2, y: 2, z: 4, core: 2. Of those that a mesh axis runs over, the one named last changes fastest.
Arguments:
- cells: bfloat16 [8192, 768], P(('row', 'blk')), may hold values from -12 to 12
- tile_rows: int32 [384], P(('row', 'blk')), may hold values from 0 to 1, as said below
- tile_cols: int32 [384], P(('row', 'blk')), may hold values from 0 to 5, as said below
- tile_count: int32 [32], P(('row', 'blk')), may hold values from 6 to 12, as said below
- halo_blocks: int32 [32], P(('row', 'blk')), may hold values from 0 to 1, as said below
- tile_vals: bfloat16 [384, 128, 128], P(('row', 'blk')), may hold values from -0.375 to 0.375
- pool_ids: int32 [8192], P(('row', 'blk')), may hold values from 0 to 15, as said below
- w_msg: bfloat16 [768, 768], replicated, may hold values from -0.21875 to 0.21875
- w_query: bfloat16 [768, 768], replicated, may hold values from -1 to 2
- cotangent: bfloat16 [8192, 768], P(('row', 'blk')), may hold values from -6 to 6
Outputs:
- passed: bfloat16 [8192, 768], P(('row', 'blk'))
- attended: bfloat16 [8192, 768], P(('row', 'blk'))
- grad_cells: bfloat16 [8192, 768], P(('row', 'blk'))
Inputs may be any that keep to these rules, and one draw needn't show every extreme that they name: `tile_rows`: slot i of a partition's 12 slots, for i < 2, has row i. `tile_cols`: slot i of a partition, for i < 6, has column i; later slots have columns below 2. `tile_count`: slots of a partition at or beyond its count are unused. `halo_blocks`: distinct within one partition. `pool_ids`: every supernode of a partition has at least one of its cells; the first two cells of a partition lie in supernodes 0 and 1.
All inputs are finite; a program needn't handle non-finite values.
Results may differ from a plain program's by a relative error of at most 0.04.
The roundings to bfloat16 on the way count: a program that leaves them out, or rounds other values in their place, can miss the bound.
Values may be sent and summed in bfloat16 or wider, within the bound.
A program may use at most 64 MiB of HBM per device.

v0:
```python
import jax
import jax.numpy as jnp
from jax import lax
from jax.sharding import PartitionSpec as P

D = 768
HEADS = 12
HEAD = 64
BLOCK = 128
NB = 2
HB = 1
SN_DEV = 16
EXT = 6
CELL_DEV = 256


def padded(value, sides, width):
    for axis, dim in sides:
        count, length = (lax.axis_size(axis), value.shape[dim])
        up = [(i, (i + 1) % count) for i in range(count - 1)]
        down = [(j, i) for i, j in up]
        last = lax.slice_in_dim(value, length - width, length, axis=dim)
        leading = lax.slice_in_dim(value, 0, width, axis=dim)
        before = lax.ppermute(last, axis, up)
        after = lax.ppermute(leading, axis, down)
        value = jnp.concatenate([before, value, after], axis=dim)
    return value


def from_behind(value, axis, by):
    count = lax.axis_size(axis)
    return lax.ppermute(value, axis, [(i, (i + by) % count) for i in range(count)])


def passed_along(value, axis, steps):
    count = lax.axis_size(axis)
    leading, last = (max(0, -steps), min(count, count - steps))
    return lax.ppermute(value, axis, [(source, source + steps) for source in range(leading, last)])


def silu_slope(values):
    sigma = jax.nn.sigmoid(values)
    return sigma * (1.0 + values * (1.0 - sigma))


def body(
    cells,
    tile_rows,
    tile_cols,
    tile_count,
    halo_blocks,
    tile_vals,
    pool_ids,
    w_msg,
    w_query,
    cotangent,
):
    blocks = cells.reshape(NB, BLOCK, D)
    boundary = blocks[halo_blocks]
    beside_all = padded(boundary[None, None], (("row", 0), ("blk", 1)), 1)
    extended = jnp.concatenate(
        [blocks, beside_all[0, 1], beside_all[2, 1], beside_all[1, 0], beside_all[1, 2]], axis=0
    )
    live_count = tile_count[0]

    def add_tile(number, totals):
        picked = lax.dynamic_index_in_dim(extended, tile_cols[number], 0, keepdims=False)
        product = jnp.dot(tile_vals[number], picked, preferred_element_type=jnp.float32)
        return totals.at[tile_rows[number]].add(product)

    msg_sums = lax.fori_loop(0, live_count, add_tile, jnp.zeros((NB, BLOCK, D), jnp.float32))
    message = msg_sums.astype(jnp.bfloat16).reshape(CELL_DEV, D)
    hidden = jnp.dot(message, w_msg, preferred_element_type=jnp.float32)
    passed = (cells.astype(jnp.float32) + jax.nn.silu(hidden)).astype(jnp.bfloat16)
    member = pool_ids[None, :] == jnp.arange(SN_DEV, dtype=jnp.int32)[:, None]
    member_bf = member.astype(jnp.bfloat16)
    counts = jnp.sum(member.astype(jnp.float32), axis=1)
    root_count = jnp.sqrt(counts)[:, None]
    pooled = jnp.dot(member_bf, passed, preferred_element_type=jnp.float32)
    supern = (pooled / root_count).astype(jnp.bfloat16)
    query_proj = jnp.dot(passed, w_query, preferred_element_type=jnp.float32).astype(jnp.bfloat16)
    key_table = lax.all_gather(supern, "blk", axis=0, tiled=True)
    score_scale = HEAD ** (-0.5)
    queries = query_proj.reshape(CELL_DEV, HEADS, HEAD)
    key_rows = key_table.reshape(-1, HEADS, HEAD)
    grads = cotangent.reshape(CELL_DEV, HEADS, HEAD)
    scores = (
        jnp.einsum("qhe,khe->hqk", queries, key_rows, preferred_element_type=jnp.float32)
        * score_scale
    )
    weights = jnp.exp(scores - jnp.max(scores, axis=2, keepdims=True))
    weights = weights / jnp.sum(weights, axis=2, keepdims=True)
    rounded = weights.astype(jnp.bfloat16)
    values_sum = jnp.einsum("hqk,khe->qhe", rounded, key_rows, preferred_element_type=jnp.float32)
    centre = jnp.sum(grads.astype(jnp.float32) * values_sum, axis=2)
    slope = jnp.einsum("qhe,khe->hqk", grads, key_rows, preferred_element_type=jnp.float32)
    dscore = (weights * (slope - centre.T[:, :, None]) * score_scale).astype(jnp.bfloat16)
    dquery = (
        jnp.einsum("hqk,khe->qhe", dscore, key_rows, preferred_element_type=jnp.float32)
        .astype(jnp.bfloat16)
        .reshape(CELL_DEV, D)
    )

    def key_terms(first_row, span_rows):
        part_score = lax.dynamic_slice_in_dim(dscore, first_row, span_rows, 2)
        part_weight = lax.dynamic_slice_in_dim(rounded, first_row, span_rows, 2)
        from_scores = jnp.einsum(
            "hqk,qhe->khe", part_score, queries, preferred_element_type=jnp.float32
        )
        from_values = jnp.einsum(
            "hqk,qhe->khe", part_weight, grads, preferred_element_type=jnp.float32
        )
        return (from_scores + from_values).reshape(span_rows, D)

    position = lax.axis_index("blk")
    loop_size = lax.axis_size("blk")
    held = key_terms((position - 1) % loop_size * SN_DEV, SN_DEV)

    def pass_along(section, carried):
        carried = from_behind(carried, "blk", 1)
        owner = (position - 1 - section) % loop_size
        return carried + key_terms(owner * SN_DEV, SN_DEV)

    key_grad = lax.fori_loop(1, loop_size, pass_along, held)
    pool_grad = (key_grad / root_count).astype(jnp.bfloat16)
    spread = jnp.einsum("sc,sf->cf", member_bf, pool_grad, preferred_element_type=jnp.float32)
    back_query = lax.dot_general(
        dquery, w_query, (((1,), (1,)), ((), ())), preferred_element_type=jnp.float32
    )
    through = (cotangent.astype(jnp.float32) + back_query + spread).astype(jnp.bfloat16)
    dhidden = (through.astype(jnp.float32) * silu_slope(hidden)).astype(jnp.bfloat16)
    dmessage = (
        lax.dot_general(
            dhidden, w_msg, (((1,), (1,)), ((), ())), preferred_element_type=jnp.float32
        )
        .astype(jnp.bfloat16)
        .reshape(NB, BLOCK, D)
    )

    def back_tile(number, totals):
        picked = lax.dynamic_index_in_dim(dmessage, tile_rows[number], 0, keepdims=False)
        product = lax.dot_general(
            tile_vals[number], picked, (((0,), (0,)), ((), ())), preferred_element_type=jnp.float32
        )
        return totals.at[tile_cols[number]].add(product)

    ext_grad = lax.fori_loop(0, live_count, back_tile, jnp.zeros((EXT, BLOCK, D), jnp.float32))
    returned = jnp.zeros((HB, BLOCK, D), jnp.float32)
    for offset, first_slot in ((1, NB + HB), (-1, NB)):
        returned = returned + passed_along(ext_grad[first_slot : first_slot + HB], "row", offset)
    for offset, first_slot in ((1, NB + 3 * HB), (-1, NB + 2 * HB)):
        returned = returned + passed_along(ext_grad[first_slot : first_slot + HB], "blk", offset)
    summed = through.astype(jnp.float32).reshape(NB, BLOCK, D) + ext_grad[:NB]
    summed = summed.at[halo_blocks].add(returned)
    attended = values_sum.astype(jnp.bfloat16).reshape(CELL_DEV, D)
    return (passed, attended, summed.astype(jnp.bfloat16).reshape(CELL_DEV, D))


def solution(mesh):
    return jax.shard_map(
        body,
        mesh=mesh,
        in_specs=(
            P(("row", "blk"), None),
            P(("row", "blk")),
            P(("row", "blk")),
            P(("row", "blk")),
            P(("row", "blk")),
            P(("row", "blk"), None, None),
            P(("row", "blk")),
            P(),
            P(),
            P(("row", "blk"), None),
        ),
        out_specs=(P(("row", "blk"), None), P(("row", "blk"), None), P(("row", "blk"), None)),
        check_vma=False,
    )
```

profile of v0, /device:TPU:0, one launch (start us, length us, event | category | flops | bytes accessed | tf_op | source)
XLA Modules:
  0.0 319.8 jit_solution(17326051294638677633)
XLA Ops:
  2.4 4.9 %collective-permute-start.1 = (bf16[1,1,1,128,768]{4,3,2,1,0:T(8,128)(2,1)S(1)}, bf16[1,1,1,128,768]{4,3,2,1,0:T(8,128)(2,1)S(1)}, u32[]{:S(2)}, u32[]{:S(2)}) collective-permute-start(bf16[1,1,1,128,768]{4,3,2,1,0:T(8,128)(2,1)S(1)} %dynamic-slice_bitcast_fusion), channel_id=1, source_target_pairs={{0,8},{8,16},{16,24},{1,9},{9,17},{17,25},{2,10},{10,18},{18,26},{... | collective-permute-start | bytes 589832 | tf_op jit(solution)/shard_map/ppermute | solution.py:24
  11.4 6.2 %collective-permute-done.2 = bf16[1,1,1,128,768]{4,3,2,1,0:T(8,128)(2,1)S(1)} collective-permute-done((bf16[1,1,1,128,768]{4,3,2,1,0:T(8,128)(2,1)S(1)}, bf16[1,1,1,128,768]{4,3,2,1,0:T(8,128)(2,1)S(1)}, u32[]{:S(2)}, u32[]{:S(2)}) %collective-permute-start.2) | collective-permute-done | bytes 196640 | tf_op jit(solution)/shard_map/ppermute | solution.py:25
  20.6 4.2 %collective-permute-done.4 = bf16[3,1,1,128,768]{4,3,2,1,0:T(8,128)(2,1)S(1)} collective-permute-done((bf16[3,1,1,128,768]{4,3,2,1,0:T(8,128)(2,1)S(1)}, bf16[3,1,1,128,768]{4,3,2,1,0:T(8,128)(2,1)S(1)}, u32[]{:S(2)}, u32[]{:S(2)}) %collective-permute-start.4) | collective-permute-done | bytes 589856 | tf_op jit(solution)/shard_map/ppermute | solution.py:25
  24.8 101.1 %while.39 = (s32[]{:T(128)}, f32[2,128,768]{2,1,0:T(8,128)S(1)}, s32[]{:T(128)}, s32[12]{0:T(128)S(1)}, bf16[12,128,128]{2,1,0:T(8,128)(2,1)}, /*index=5*/s32[12...) while((s32[]{:T(128)}, f32[2,128,768]{2,1,0:T(8,128)S(1)}, ...), condition=%wide.region_2.3_spmd, body=%wide.region_0.2_spmd.sunk | while | flops 25362460 | bytes 1017128 | solution.py:71
  128.5 20.8 %all_gather.3 = bf16[128,768]{1,0:T(8,128)(2,1)} all-gather(bf16[16,768]{1,0:T(8,128)(2,1)S(1)} %fusion.30), channel_id=1, replica_groups=mesh['row'=4,'blk'=8] {'blk'}, dimensions={0}, use_global_device_ids=true | all-gather | bytes 221184 | tf_op jit(solution)/shard_map/all_gather | solution.py:82
  152.8 1.8 fusion.47
  161.7 37.6 %while.40 = (s32[]{:T(128)}, f32[16,768]{1,0:T(8,128)S(1)}, s32[]{:T(128)}, bf16[12,256,128]{1,2,0:T(8,128)(2,1)}, bf16[256,12,64]{0,2,1:T(8,128)(2,1)S(1)}, /*i...) while((s32[]{:T(128)}, f32[16,768]{1,0:T(8,128)S(1)}, ...), condition=%wide.region_8.9_spmd, body=%wide.region_7.8_spmd.sunk | while | flops 12607506 | bytes 1720660 | solution.py:124
  163.6 3.5 %collective-permute-done = f32[16,768]{1,0:T(8,128)S(1)} collective-permute-done((f32[16,768]{1,0:T(8,128)S(1)}, f32[16,768]{1,0:T(8,128)S(1)}, u32[]{:S(2)}, u32[]{:S(2)}) %collective-permute-start) | collective-permute-done | bytes 49184 | tf_op jit(solution)/shard_map/while/body/eval_jaxpr/ppermute | solution.py:32
  168.7 3.8 %collective-permute-done = f32[16,768]{1,0:T(8,128)S(1)} collective-permute-done((f32[16,768]{1,0:T(8,128)S(1)}, f32[16,768]{1,0:T(8,128)S(1)}, u32[]{:S(2)}, u32[]{:S(2)}) %collective-permute-start) | collective-permute-done | bytes 49184 | tf_op jit(solution)/shard_map/while/body/eval_jaxpr/ppermute | solution.py:32
  174.0 3.8 %collective-permute-done = f32[16,768]{1,0:T(8,128)S(1)} collective-permute-done((f32[16,768]{1,0:T(8,128)S(1)}, f32[16,768]{1,0:T(8,128)S(1)}, u32[]{:S(2)}, u32[]{:S(2)}) %collective-permute-start) | collective-permute-done | bytes 49184 | tf_op jit(solution)/shard_map/while/body/eval_jaxpr/ppermute | solution.py:32
  179.4 3.8 %collective-permute-done = f32[16,768]{1,0:T(8,128)S(1)} collective-permute-done((f32[16,768]{1,0:T(8,128)S(1)}, f32[16,768]{1,0:T(8,128)S(1)}, u32[]{:S(2)}, u32[]{:S(2)}) %collective-permute-start) | collective-permute-done | bytes 49184 | tf_op jit(solution)/shard_map/while/body/eval_jaxpr/ppermute | solution.py:32
  184.8 3.8 %collective-permute-done = f32[16,768]{1,0:T(8,128)S(1)} collective-permute-done((f32[16,768]{1,0:T(8,128)S(1)}, f32[16,768]{1,0:T(8,128)S(1)}, u32[]{:S(2)}, u32[]{:S(2)}) %collective-permute-start) | collective-permute-done | bytes 49184 | tf_op jit(solution)/shard_map/while/body/eval_jaxpr/ppermute | solution.py:32
  190.1 3.8 %collective-permute-done = f32[16,768]{1,0:T(8,128)S(1)} collective-permute-done((f32[16,768]{1,0:T(8,128)S(1)}, f32[16,768]{1,0:T(8,128)S(1)}, u32[]{:S(2)}, u32[]{:S(2)}) %collective-permute-start) | collective-permute-done | bytes 49184 | tf_op jit(solution)/shard_map/while/body/eval_jaxpr/ppermute | solution.py:32
  195.5 3.8 %collective-permute-done = f32[16,768]{1,0:T(8,128)S(1)} collective-permute-done((f32[16,768]{1,0:T(8,128)S(1)}, f32[16,768]{1,0:T(8,128)S(1)}, u32[]{:S(2)}, u32[]{:S(2)}) %collective-permute-start) | collective-permute-done | bytes 49184 | tf_op jit(solution)/shard_map/while/body/eval_jaxpr/ppermute | solution.py:32
  203.0 93.1 %while.41 = (s32[]{:T(128)}, f32[6,128,768]{2,1,0:T(8,128)S(1)}, s32[]{:T(128)}, s32[12]{0:T(128)S(1)}, bf16[12,128,128]{2,1,0:T(8,128)(2,1)}, /*index=5*/s32[12...) while((s32[]{:T(128)}, f32[6,128,768]{2,1,0:T(8,128)S(1)}, ...), condition=%wide.region_11.12_spmd, body=%wide.region_9.11_spmd.sunk | while | flops 25362460 | bytes 1017128 | solution.py:147
  224.3 1.8 fusion.91
  232.0 1.8 fusion.91
  278.3 1.8 fusion.91
  298.5 3.8 %collective-permute-start.7 = (f32[1,128,768]{2,1,0:T(8,128)}, f32[1,128,768]{2,1,0:T(8,128)}, u32[]{:S(2)}, u32[]{:S(2)}) collective-permute-start(f32[1,128,768]{2,1,0:T(8,128)} %get-tuple-element.369), channel_id=1, source_target_pairs={{0,1},{1,2},{2,3},{3,4},{4,5},{5,6},{6,7},{8,9},{9,10},{10,11},{11... | collective-permute-start | bytes 1179656 | tf_op jit(solution)/shard_map/ppermute | solution.py:38
  302.4 2.0 collective-permute-start.5
  306.5 1.9 copy.39
  309.6 2.4 collective-permute-done.5
  312.0 4.8 %collective-permute-done.6 = f32[1,128,768]{2,1,0:T(8,128)} collective-permute-done((f32[1,128,768]{2,1,0:T(8,128)}, f32[1,128,768]{2,1,0:T(8,128)}, u32[]{:S(2)}, u32[]{:S(2)}) %collective-permute-start.6) | collective-permute-done | bytes 393248 | tf_op jit(solution)/shard_map/ppermute | solution.py:38
  316.9 2.2 fusion.32
  (209 shorter events, 128.9 us)
Async XLA Ops:
  0.6 125.4 %copy-start = (bf16[768,768]{1,0:T(8,128)(2,1)S(1)}, bf16[768,768]{1,0:T(8,128)(2,1)}, u32[]{:S(2)}) copy-start(bf16[768,768]{1,0:T(8,128)(2,1)} %param.29) | copy-start | bytes 3538948
  0.6 9.1 %copy-start.12 = (s32[256]{0:T(256)S(1)}, s32[256]{0:T(256)}, u32[]{:S(2)}) copy-start(s32[256]{0:T(256)} %param.28) | copy-start | bytes 3076
  1.4 17.6 %copy-start.8 = (bf16[256,768]{1,0:T(8,128)(2,1)S(1)}, bf16[256,768]{1,0:T(8,128)(2,1)}, u32[]{:S(2)}) copy-start(bf16[256,768]{1,0:T(8,128)(2,1)} %param.22) | copy-start | bytes 1179652
  2.4 9.0 %collective-permute-start.1 = (bf16[1,1,1,128,768]{4,3,2,1,0:T(8,128)(2,1)S(1)}, bf16[1,1,1,128,768]{4,3,2,1,0:T(8,128)(2,1)S(1)}, u32[]{:S(2)}, u32[]{:S(2)}) collective-permute-start(bf16[1,1,1,128,768]{4,3,2,1,0:T(8,128)(2,1)S(1)} %dynamic-slice_bitcast_fusion), channel_id=1, source_target_pairs={{0,8},{8,16},{16,24},{1,9},{9,17},{17,25},{2,10},{10,18},{18,26},{... | collective-permute-start | bytes 589832 | tf_op jit(solution)/shard_map/ppermute | solution.py:24
  7.3 10.3 %collective-permute-start.2 = (bf16[1,1,1,128,768]{4,3,2,1,0:T(8,128)(2,1)S(1)}, bf16[1,1,1,128,768]{4,3,2,1,0:T(8,128)(2,1)S(1)}, u32[]{:S(2)}, u32[]{:S(2)}) collective-permute-start(bf16[1,1,1,128,768]{4,3,2,1,0:T(8,128)(2,1)S(1)} %dynamic-slice_bitcast_fusion), channel_id=1, source_target_pairs={{8,0},{16,8},{24,16},{9,1},{17,9},{25,17},{10,2},{18,10},{26,18},{... | collective-permute-start | bytes 589832 | tf_op jit(solution)/shard_map/ppermute | solution.py:25
  17.7 2.9 collective-permute-start.3
  19.0 5.8 %copy-start.10 = (s32[3]{0:T(128)S(1)}, s32[3]{0:T(128)}, u32[]{:S(2)}) copy-start(s32[3]{0:T(128)} %constant.195.clone.1) | copy-start | bytes 40
  19.0 5.8 %copy-start.13 = (s32[12]{0:T(128)S(1)}, s32[12]{0:T(128)}, u32[]{:S(2)}) copy-start(s32[12]{0:T(128)} %param.23) | copy-start | bytes 148
  19.1 5.7 %collective-permute-start.4 = (bf16[3,1,1,128,768]{4,3,2,1,0:T(8,128)(2,1)S(1)}, bf16[3,1,1,128,768]{4,3,2,1,0:T(8,128)(2,1)S(1)}, u32[]{:S(2)}, u32[]{:S(2)}) collective-permute-start(bf16[3,1,1,128,768]{4,3,2,1,0:T(8,128)(2,1)S(1)} %pad_maximum_fusion), channel_id=1, source_target_pairs={{1,0},{2,1},{3,2},{4,3},{5,4},{6,5},{7,6},{9,8},{10,9},{11,10},{12... | collective-permute-start | bytes 1769480 | tf_op jit(solution)/shard_map/ppermute | solution.py:25
  127.0 23.4 %copy-start.1 = (bf16[768,768]{1,0:T(8,128)(2,1)S(1)}, bf16[768,768]{1,0:T(8,128)(2,1)}, u32[]{:S(2)}) copy-start(bf16[768,768]{1,0:T(8,128)(2,1)} %param.30) | copy-start | bytes 3538948
  128.3 23.3 %copy-start.7 = (bf16[256,768]{1,0:T(8,128)(2,1)}, bf16[256,768]{1,0:T(8,128)(2,1)S(1)}, u32[]{:S(2)}) copy-start(bf16[256,768]{1,0:T(8,128)(2,1)S(1)} %get-tuple-element.373) | copy-start | bytes 1179652
  158.1 3.0 copy-start.4
  161.7 5.4 %collective-permute-start = (f32[16,768]{1,0:T(8,128)S(1)}, f32[16,768]{1,0:T(8,128)S(1)}, u32[]{:S(2)}, u32[]{:S(2)}) collective-permute-start(f32[16,768]{1,0:T(8,128)S(1)} %get-tuple-element.565), channel_id=1, source_target_pairs={{0,1},{1,2},{2,3},{3,4},{4,5},{5,6},{6,7},{7,0},{8,9},{9,10},{10,1... | collective-permute-start | bytes 147464 | tf_op jit(solution)/shard_map/while/body/eval_jaxpr/ppermute | solution.py:32
  167.1 5.4 %collective-permute-start = (f32[16,768]{1,0:T(8,128)S(1)}, f32[16,768]{1,0:T(8,128)S(1)}, u32[]{:S(2)}, u32[]{:S(2)}) collective-permute-start(f32[16,768]{1,0:T(8,128)S(1)} %get-tuple-element.565), channel_id=1, source_target_pairs={{0,1},{1,2},{2,3},{3,4},{4,5},{5,6},{6,7},{7,0},{8,9},{9,10},{10,1... | collective-permute-start | bytes 147464 | tf_op jit(solution)/shard_map/while/body/eval_jaxpr/ppermute | solution.py:32
  172.5 5.4 %collective-permute-start = (f32[16,768]{1,0:T(8,128)S(1)}, f32[16,768]{1,0:T(8,128)S(1)}, u32[]{:S(2)}, u32[]{:S(2)}) collective-permute-start(f32[16,768]{1,0:T(8,128)S(1)} %get-tuple-element.565), channel_id=1, source_target_pairs={{0,1},{1,2},{2,3},{3,4},{4,5},{5,6},{6,7},{7,0},{8,9},{9,10},{10,1... | collective-permute-start | bytes 147464 | tf_op jit(solution)/shard_map/while/body/eval_jaxpr/ppermute | solution.py:32
  177.8 5.4 %collective-permute-start = (f32[16,768]{1,0:T(8,128)S(1)}, f32[16,768]{1,0:T(8,128)S(1)}, u32[]{:S(2)}, u32[]{:S(2)}) collective-permute-start(f32[16,768]{1,0:T(8,128)S(1)} %get-tuple-element.565), channel_id=1, source_target_pairs={{0,1},{1,2},{2,3},{3,4},{4,5},{5,6},{6,7},{7,0},{8,9},{9,10},{10,1... | collective-permute-start | bytes 147464 | tf_op jit(solution)/shard_map/while/body/eval_jaxpr/ppermute | solution.py:32
  183.2 5.4 %collective-permute-start = (f32[16,768]{1,0:T(8,128)S(1)}, f32[16,768]{1,0:T(8,128)S(1)}, u32[]{:S(2)}, u32[]{:S(2)}) collective-permute-start(f32[16,768]{1,0:T(8,128)S(1)} %get-tuple-element.565), channel_id=1, source_target_pairs={{0,1},{1,2},{2,3},{3,4},{4,5},{5,6},{6,7},{7,0},{8,9},{9,10},{10,1... | collective-permute-start | bytes 147464 | tf_op jit(solution)/shard_map/while/body/eval_jaxpr/ppermute | solution.py:32
  188.6 5.4 %collective-permute-start = (f32[16,768]{1,0:T(8,128)S(1)}, f32[16,768]{1,0:T(8,128)S(1)}, u32[]{:S(2)}, u32[]{:S(2)}) collective-permute-start(f32[16,768]{1,0:T(8,128)S(1)} %get-tuple-element.565), channel_id=1, source_target_pairs={{0,1},{1,2},{2,3},{3,4},{4,5},{5,6},{6,7},{7,0},{8,9},{9,10},{10,1... | collective-permute-start | bytes 147464 | tf_op jit(solution)/shard_map/while/body/eval_jaxpr/ppermute | solution.py:32
  194.0 5.4 %collective-permute-start = (f32[16,768]{1,0:T(8,128)S(1)}, f32[16,768]{1,0:T(8,128)S(1)}, u32[]{:S(2)}, u32[]{:S(2)}) collective-permute-start(f32[16,768]{1,0:T(8,128)S(1)} %get-tuple-element.565), channel_id=1, source_target_pairs={{0,1},{1,2},{2,3},{3,4},{4,5},{5,6},{6,7},{7,0},{8,9},{9,10},{10,1... | collective-permute-start | bytes 147464 | tf_op jit(solution)/shard_map/while/body/eval_jaxpr/ppermute | solution.py:32
  200.9 1.6 copy-start.3
  297.3 12.3 %collective-permute-start.8 = (f32[1,128,768]{2,1,0:T(8,128)}, f32[1,128,768]{2,1,0:T(8,128)}, u32[]{:S(2)}, u32[]{:S(2)}) collective-permute-start(f32[1,128,768]{2,1,0:T(8,128)} %get-tuple-element.368), channel_id=1, source_target_pairs={{1,0},{2,1},{3,2},{4,3},{5,4},{6,5},{7,6},{9,8},{10,9},{11,10},{12... | collective-permute-start | bytes 1179656 | tf_op jit(solution)/shard_map/ppermute | solution.py:38
  298.5 11.1 %collective-permute-start.7 = (f32[1,128,768]{2,1,0:T(8,128)}, f32[1,128,768]{2,1,0:T(8,128)}, u32[]{:S(2)}, u32[]{:S(2)}) collective-permute-start(f32[1,128,768]{2,1,0:T(8,128)} %get-tuple-element.369), channel_id=1, source_target_pairs={{0,1},{1,2},{2,3},{3,4},{4,5},{5,6},{6,7},{8,9},{9,10},{10,11},{11... | collective-permute-start | bytes 1179656 | tf_op jit(solution)/shard_map/ppermute | solution.py:38
  302.4 9.7 %collective-permute-start.5 = (f32[1,128,768]{2,1,0:T(8,128)}, f32[1,128,768]{2,1,0:T(8,128)}, u32[]{:S(2)}, u32[]{:S(2)}) collective-permute-start(f32[1,128,768]{2,1,0:T(8,128)} %get-tuple-element.370), channel_id=1, source_target_pairs={{0,8},{8,16},{16,24},{1,9},{9,17},{17,25},{2,10},{10,18},{18,26},{... | collective-permute-start | bytes 1179656 | tf_op jit(solution)/shard_map/ppermute | solution.py:38
  304.4 12.5 %collective-permute-start.6 = (f32[1,128,768]{2,1,0:T(8,128)}, f32[1,128,768]{2,1,0:T(8,128)}, u32[]{:S(2)}, u32[]{:S(2)}) collective-permute-start(f32[1,128,768]{2,1,0:T(8,128)} %get-tuple-element.367), channel_id=1, source_target_pairs={{8,0},{16,8},{24,16},{9,1},{17,9},{25,17},{10,2},{18,10},{26,18},{... | collective-permute-start | bytes 1179656 | tf_op jit(solution)/shard_map/ppermute | solution.py:38
  (7 other events, 8.0 us)
where the time goes:
time: 325 us; the launch traced here: 320 us
  loops' own time  103 us (32%)
  matrix products  59.6 us (18%)
  local copies, waits for them, and re-layouts  48 us (15%)
  waiting for transfers between devices  45.6 us (14%)
  other arithmetic  23.6 us (7%)
  blocking collectives  20.8 us (6%)
  starting transfers between devices  17.9 us (6%)
    another operation x1, loops' own time, body(): lax.fori_loop(0, live_count, add_tile, jnp.zeros((NB, BLOCK, D), jnp.floa...  52.6 us
    another operation x1, loops' own time, body(): lax.fori_loop(0, live_count, back_tile, jnp.zeros((EXT, BLOCK, D), jnp.fl...  49.7 us
    ppermute x7, waiting for transfers between devices, from_behind(): lax.ppermute(value, axis, [(i, (i + by) % count) for i in range(count)])  26.4 us
    dot_general x12, matrix products, back_tile(): lax.dot_general(tile_vals[number], picked, (((0,), (0,)), ((), ())), pref...  21.1 us
    all_gather x1, blocking collectives, body(): key_table = lax.all_gather(supern, 'blk', axis=0, tiled=True)  20.8 us
    dot_general x12, matrix products, add_tile(): jnp.dot(tile_vals[number], picked, preferred_element_type=jnp.float32)  18.3 us
    another operation x25, other arithmetic  17.6 us
    dynamic_slice x12, local copies, waits for them, and re-layouts, add_tile(): tile_cols[number]  14.8 us
  transfers between devices with their start and end apart: 15, of which 13 were waited for; matrix products, arithmetic and copies ran while one was open for 5% of the time, Pallas kernels for 0%

commit v1 on v0

v1 whole, which is shorter than its diff:
```python
import functools

import jax
import jax.numpy as jnp
from jax import lax
from jax.experimental import pallas as pl
from jax.experimental.pallas import tpu as pltpu
from jax.sharding import PartitionSpec as P

D = 768
HEAD = 64
BLOCK = 128
NB = 2
SN_DEV = 16
EXT = 6
TILES = 12
CELL_DEV = 256
PAIR = 2 * HEAD
CHUNK = 256
CHUNKS = D // CHUNK
LOG2E = 1.4426950408889634
BF = jnp.bfloat16
F32 = jnp.float32
MESH = pl.DeviceIdType.MESH


def dot(a, b):
    return jnp.dot(a, b, preferred_element_type=F32)


def dot_nt(a, b):
    return lax.dot_general(a, b, (((1,), (1,)), ((), ())), preferred_element_type=F32)


def cols(j, width=CHUNK):
    return slice(j * width, (j + 1) * width)


def kernel(
    n_row, n_blk,
    cells, rows, colsr, count, halo, tiles, pool, w_msg, w_query, cot,
    passed_o, att_o, grad_o,
    ext, bnd, tv, wm, wq, cv, adj, adj_lo, adj_t, wm_t, wq_t, msg, hid, sig, pas, qry, keys,
    att, dqr, kg, kgr, gs, gr, own, out, dh, base, dm, via,
    lc, ld, st, hs, hr, ks, kr, ps, pr, ss, sr, vr, vs,
):
    r = lax.axis_index("row")
    c = lax.axis_index("blk")
    nk = SN_DEV * n_blk

    loads = [
        pltpu.make_async_copy(tiles, tv, ld.at[1]),
        pltpu.make_async_copy(w_msg, wm, ld.at[2]),
        pltpu.make_async_copy(w_query, wq, ld.at[3]),
        pltpu.make_async_copy(cot, cv, ld.at[4]),
    ]
    cell_loads = [
        pltpu.make_async_copy(cells.at[:, pl.ds(j * CHUNK, CHUNK)], ext.at[j, pl.ds(0, CELL_DEV)], lc.at[j])
        for j in range(CHUNKS)
    ]
    for load in cell_loads + loads:
        load.start()

    barrier = pltpu.get_barrier_semaphore()
    for off in range(1, n_blk):
        pl.semaphore_signal(
            barrier, inc=1, device_id=(r, lax.rem(c + off, n_blk)), device_id_type=MESH
        )

    has_up, has_down = r > 0, r < n_row - 1
    has_left, has_right = c > 0, c < n_blk - 1
    up, down = jnp.maximum(r - 1, 0), jnp.minimum(r + 1, n_row - 1)
    left, right = jnp.maximum(c - 1, 0), jnp.minimum(c + 1, n_blk - 1)

    relay = n_row == 4
    if relay:
        middle = jnp.where(lax.rem(c, 2) == 0, 0, n_row - 1)
        hands_on = r == middle
        diagonal = (r == 2, r == 1)
        for off in range(1, n_row):
            pl.semaphore_signal(
                barrier, inc=1, device_id=(lax.rem(r + off, n_row), c), device_id_type=MESH
            )
        greeted = (n_blk - 1) + (n_row - 1)
    else:
        @pl.when(has_up)
        def _():
            pl.semaphore_signal(barrier, inc=1, device_id=(up, c), device_id_type=MESH)

        @pl.when(has_down)
        def _():
            pl.semaphore_signal(barrier, inc=1, device_id=(down, c), device_id_type=MESH)

        greeted = (n_blk - 1) + has_up.astype(jnp.int32) + has_down.astype(jnp.int32)

    sides = (
        (has_up, (up, c)),
        (has_down, (down, c)),
        (has_left, (r, left)),
        (has_right, (r, right)),
    )

    def halo_send(j, s):
        there = NB + (s ^ 1)
        return pltpu.make_async_remote_copy(
            src_ref=bnd.at[j],
            dst_ref=ext.at[j, pl.ds(there * BLOCK, BLOCK)],
            send_sem=hs.at[j, s],
            recv_sem=hr.at[j, s ^ 1],
            device_id=sides[s][1],
            device_id_type=MESH,
        )

    def straight(s):
        if relay and s < 2:
            return sides[s][0] & jnp.logical_not(diagonal[s])
        return sides[s][0]

    def to_middle(phase, part, sem, j, s):
        return pltpu.make_async_remote_copy(
            src_ref=part,
            dst_ref=via.at[phase, j, s],
            send_sem=sem.at[j, s],
            recv_sem=vr.at[phase, j, s],
            device_id=(middle, c),
            device_id_type=MESH,
        )

    def from_middle(phase, j, s):
        if phase == 0:
            there = ext.at[j, pl.ds((NB + (s ^ 1)) * BLOCK, BLOCK)]
            sem = hr.at[j, s ^ 1]
        else:
            there = gr.at[j, s ^ 1]
            sem = sr.at[j, s ^ 1]
        return pltpu.make_async_remote_copy(
            src_ref=via.at[phase, j, s],
            dst_ref=there,
            send_sem=vs.at[phase, j, s],
            recv_sem=sem,
            device_id=((1, 2)[s], c),
            device_id_type=MESH,
        )

    def hand_on(phase, j):
        if relay:
            for s in (0, 1):
                @pl.when(hands_on)
                def _():
                    to_middle(phase, bnd.at[j], hs, j, s).wait_recv()
                    from_middle(phase, j, s).start()

    def halo_recv(j, s):
        return pltpu.make_async_remote_copy(
            src_ref=bnd.at[j],
            dst_ref=ext.at[j, pl.ds((NB + s) * BLOCK, BLOCK)],
            send_sem=hs.at[j, s],
            recv_sem=hr.at[j, s],
            device_id=sides[s][1],
            device_id_type=MESH,
        )

    def key_copy(j, off):
        return pltpu.make_async_remote_copy(
            src_ref=keys.at[j, pl.ds(pl.multiple_of(c * SN_DEV, SN_DEV), SN_DEV)],
            dst_ref=keys.at[j, pl.ds(pl.multiple_of(c * SN_DEV, SN_DEV), SN_DEV)],
            send_sem=ks.at[j, off],
            recv_sem=kr.at[j, off],
            device_id=(r, lax.rem(c + off, n_blk)),
            device_id_type=MESH,
        )

    def key_recv(j, off):
        source = lax.rem(c + n_blk - off, n_blk)
        part = keys.at[j, pl.ds(pl.multiple_of(source * SN_DEV, SN_DEV), SN_DEV)]
        return pltpu.make_async_remote_copy(
            src_ref=part, dst_ref=part, send_sem=ks.at[j, off], recv_sem=kr.at[j, off],
            device_id=(r, source), device_id_type=MESH,
        )

    def part_copy(j, off):
        peer = lax.rem(c + off, n_blk)
        return pltpu.make_async_remote_copy(
            src_ref=kg.at[j, pl.ds(pl.multiple_of(peer * SN_DEV, SN_DEV), SN_DEV)],
            dst_ref=kgr.at[j, off],
            send_sem=ps.at[j, off],
            recv_sem=pr.at[j, off],
            device_id=(r, peer),
            device_id_type=MESH,
        )

    def grad_send(j, s):
        return pltpu.make_async_remote_copy(
            src_ref=gs.at[j, s],
            dst_ref=gr.at[j, s ^ 1],
            send_sem=ss.at[j, s],
            recv_sem=sr.at[j, s ^ 1],
            device_id=sides[s][1],
            device_id_type=MESH,
        )

    def grad_recv(j, s):
        return pltpu.make_async_remote_copy(
            src_ref=gs.at[j, s],
            dst_ref=gr.at[j, s],
            send_sem=ss.at[j, s],
            recv_sem=sr.at[j, s],
            device_id=sides[s][1],
            device_id_type=MESH,
        )

    second = (halo[0] == 1).astype(F32)
    for j in range(CHUNKS):
        cell_loads[j].wait()
        bnd[j] = (
            ext[j, :BLOCK].astype(F32) * (1.0 - second)
            + ext[j, BLOCK:CELL_DEV].astype(F32) * second
        ).astype(BF)
    pl.semaphore_wait(barrier, greeted)
    if relay:
        for j in range(CHUNKS):
            for s in (0, 1):
                @pl.when(diagonal[s])
                def _():
                    to_middle(0, bnd.at[j], hs, j, s).start()
    for j in range(CHUNKS):
        for s in range(4):
            @pl.when(straight(s))
            def _():
                halo_send(j, s).start()

            @pl.when(jnp.logical_not(sides[s][0]))
            def _():
                ext[j, (NB + s) * BLOCK : (NB + s + 1) * BLOCK] = jnp.zeros((BLOCK, CHUNK), BF)
                gr[j, s] = jnp.zeros((BLOCK, CHUNK), BF)

    loads[0].wait()
    live = count[0]
    for i in range(NB):
        at = slice(i * BLOCK, (i + 1) * BLOCK)
        for k in range(NB):
            total = tv[k].astype(F32) if i == k else jnp.zeros((BLOCK, BLOCK), F32)
            for s in range(EXT, TILES):
                use = (live > s) & (rows[s] == i) & (colsr[s] == k)
                total = total + tv[s].astype(F32) * use.astype(F32)
            high = total.astype(BF)
            adj[at, k * BLOCK : (k + 1) * BLOCK] = high
            adj_lo[at, k * BLOCK : (k + 1) * BLOCK] = (total - high.astype(F32)).astype(BF)
        for k in range(NB, EXT):
            use = (rows[k] == i).astype(F32)
            adj[at, k * BLOCK : (k + 1) * BLOCK] = (tv[k].astype(F32) * use).astype(BF)
    for k in range(CHUNKS):
        adj_t[cols(k), :] = adj[:, cols(k)].T
    for j in range(CHUNKS):
        own_cells = ext[j, :CELL_DEV]
        msg[:, cols(j)] = dot(adj[:, :CELL_DEV], own_cells) + dot(adj_lo[...], own_cells)
    ids = pool[...]
    member = (ids == lax.broadcasted_iota(jnp.int32, (SN_DEV, CELL_DEV), 0)).astype(F32)
    member_b = member.astype(BF)
    wide = (ids == lax.broadcasted_iota(jnp.int32, (PAIR, CELL_DEV), 0)).astype(F32)
    member_t = wide.T.astype(BF)
    root = jnp.sqrt(jnp.sum(member, axis=1, keepdims=True))
    loads[1].wait()
    loads[2].wait()
    for j in range(CHUNKS):
        hand_on(0, j)
        for k in range(CHUNKS):
            wm_t[cols(k), cols(j)] = wm[cols(j), cols(k)].T
            wq_t[cols(k), cols(j)] = wq[cols(j), cols(k)].T
    loads[3].wait()

    for j in range(CHUNKS):
        for s in (2, 3):
            @pl.when(sides[s][0])
            def _():
                halo_recv(j, s).wait_recv()
        msg[:, cols(j)] += dot(adj[:, 2 * CELL_DEV :], ext[j, 2 * CELL_DEV :])
    for j in range(CHUNKS):
        for s in (0, 1):
            @pl.when(sides[s][0])
            def _():
                halo_recv(j, s).wait_recv()
        part = (
            msg[:, cols(j)]
            + dot(adj[:, CELL_DEV : 2 * CELL_DEV], ext[j, CELL_DEV : 2 * CELL_DEV])
        ).astype(BF)
        if j == CHUNKS - 1:
            break
        for k in range(CHUNKS):
            term = dot(part, wm[cols(j), cols(k)])
            hid[:, cols(k)] = term if j == 0 else hid[:, cols(k)] + term
    mine = pl.ds(pl.multiple_of(c * SN_DEV, SN_DEV), SN_DEV)
    for j in range(CHUNKS):
        hidden = hid[:, cols(j)] + dot(part, wm[cols(CHUNKS - 1), cols(j)])
        sigma = jax.nn.sigmoid(hidden)
        hid[:, cols(j)] = hidden
        sig[:, cols(j)] = sigma
        passed = (ext[j, :CELL_DEV].astype(F32) + hidden * sigma).astype(BF)
        pas[:, cols(j)] = passed
        keys[j, mine] = (dot(member_b, passed) / root).astype(BF)
        for off in range(1, n_blk):
            key_copy(j, off).start()
    stores = [pltpu.make_async_copy(pas, passed_o, st.at[0])]
    stores[0].start()
    for j in range(CHUNKS):
        qry[:, cols(j)] = dot(pas[...], wq[:, cols(j)]).astype(BF)

    lane = lax.broadcasted_iota(jnp.int32, (1, PAIR), 1)
    even_f = (lane < HEAD).astype(F32)
    even, odd = even_f.astype(BF), (1.0 - even_f).astype(BF)
    scale = HEAD ** (-0.5)
    per = CHUNK // PAIR
    for t in range(D // PAIR):
        at = cols(t, PAIR)
        group, inner = t // per, cols(t % per, PAIR)
        if t % per == 0:
            for off in range(1, n_blk):
                key_recv(group, off).wait_recv()
        kp = keys[group, :, inner]
        k2 = jnp.concatenate([kp * even, kp * odd], axis=0)
        qp, cp = qry[:, at], cv[:, at]
        scores = dot_nt(k2, qp).reshape(2, nk, CELL_DEV)
        slope = dot_nt(k2, cp).reshape(2, nk, CELL_DEV)
        top = jnp.max(scores, axis=1, keepdims=True)
        probs = jnp.exp2((scores - top) * (scale * LOG2E))
        probs = probs * (1.0 / jnp.sum(probs, axis=1, keepdims=True))
        rounded = probs.astype(BF)
        centre = jnp.sum(rounded.astype(F32) * slope, axis=1, keepdims=True)
        dscore = (probs * (slope - centre) * scale).astype(BF)
        rounded = rounded.reshape(2 * nk, CELL_DEV)
        dscore = dscore.reshape(2 * nk, CELL_DEV)
        both = dot(dscore, qp) + dot(rounded, cp)
        kg[group, :, inner] = jnp.where(lane < HEAD, both[:nk], both[nk:]).astype(BF)
        if t % per == per - 1:
            for off in range(1, n_blk):
                part_copy(group, off).start()
        att[:, at] = dot(rounded.T, k2).astype(BF)
        dqr[:, at] = dot(dscore.T, k2).astype(BF)
    stores.append(pltpu.make_async_copy(att, att_o, st.at[1]))
    stores[1].start()
    for j in range(CHUNKS):
        base[:, cols(j)] = cv[:, cols(j)].astype(F32) + dot(dqr[...], wq_t[:, cols(j)])
        sigma = sig[:, cols(j)]
        sig[:, cols(j)] = sigma * (1.0 + hid[:, cols(j)] * (1.0 - sigma))
    for j in range(CHUNKS):
        total = kg[j, mine].astype(F32)
        for off in range(1, n_blk):
            part_copy(j, off).wait_recv()
            total = total + kgr[j, off].astype(F32)
        spread = dot(member_t[:, :SN_DEV], (total / root).astype(BF))
        through = (base[:, cols(j)] + spread).astype(BF).astype(F32)
        base[:, cols(j)] = through
        dh[:, cols(j)] = (through * sig[:, cols(j)]).astype(BF)
    for j in range(CHUNKS):
        dmsg = dot(dh[...], wm_t[:, cols(j)]).astype(BF)
        dm[:, cols(j)] = dmsg
        back = dot(adj_t[CELL_DEV:, :], dmsg)
        for s in range(4):
            gs[j, s] = back[s * BLOCK : (s + 1) * BLOCK].astype(BF)
        if relay:
            for s in (0, 1):
                @pl.when(diagonal[s])
                def _():
                    to_middle(1, gs.at[j, s], ss, j, s).start()
        for s in range(4):
            @pl.when(straight(s))
            def _():
                grad_send(j, s).start()
    for j in range(CHUNKS):
        hand_on(1, j)
        own[:, cols(j)] = base[:, cols(j)] + dot(adj_t[:CELL_DEV, :], dm[:, cols(j)])
    for j in range(CHUNKS):
        for s in (2, 3, 0, 1):
            @pl.when(sides[s][0])
            def _():
                grad_recv(j, s).wait_recv()
        returned = (
            gr[j, 0].astype(F32) + gr[j, 1].astype(F32)
            + gr[j, 2].astype(F32) + gr[j, 3].astype(F32)
        )
        out[:BLOCK, cols(j)] = (own[:BLOCK, cols(j)] + returned * (1.0 - second)).astype(BF)
        out[BLOCK:, cols(j)] = (own[BLOCK:, cols(j)] + returned * second).astype(BF)
    stores.append(pltpu.make_async_copy(out, grad_o, st.at[2]))
    stores[2].start()

    for s in range(4):
        @pl.when(straight(s))
        def _():
            for j in range(CHUNKS):
                halo_send(j, s).wait_send()
                grad_send(j, s).wait_send()
    if relay:
        for s in (0, 1):
            @pl.when(diagonal[s])
            def _():
                for j in range(CHUNKS):
                    to_middle(0, bnd.at[j], hs, j, s).wait_send()
                    to_middle(1, gs.at[j, s], ss, j, s).wait_send()

            @pl.when(hands_on)
            def _():
                for j in range(CHUNKS):
                    from_middle(0, j, s).wait_send()
                    from_middle(1, j, s).wait_send()
    for off in range(1, n_blk):
        for j in range(CHUNKS):
            key_copy(j, off).wait_send()
            part_copy(j, off).wait_send()
    for store in stores:
        store.wait()


def hand_over(a, b, c, a_o, b_o, c_o, sems):
    half = CELL_DEV // 2
    copies = [
        pltpu.make_async_copy(
            source.at[pl.ds(k * half, half)], target.at[pl.ds(k * half, half)], sems.at[i, k]
        )
        for i, (source, target) in enumerate(((a, a_o), (b, b_o), (c, c_o)))
        for k in range(2)
    ]
    for copy in copies:
        copy.start()
    for copy in copies:
        copy.wait()


def body(n_row, n_blk, cells, tile_rows, tile_cols, tile_count, halo_blocks, tile_vals, pool_ids,
         w_msg, w_query, cotangent):
    any_spec = pl.BlockSpec(memory_space=pl.ANY)
    smem = pl.BlockSpec(memory_space=pltpu.SMEM)
    vmem = pl.BlockSpec(memory_space=pltpu.VMEM)
    nk = SN_DEV * n_blk
    whole = (CELL_DEV, D)
    sem = pltpu.SemaphoreType.DMA
    results = pl.pallas_call(
        functools.partial(kernel, n_row, n_blk),
        out_shape=[jax.ShapeDtypeStruct(whole, BF)] * 3,
        in_specs=[any_spec, smem, smem, smem, smem, any_spec, vmem, any_spec, any_spec, any_spec],
        out_specs=[any_spec] * 3,
        scratch_shapes=[
            pltpu.VMEM((CHUNKS, EXT * BLOCK, CHUNK), BF),
            pltpu.VMEM((CHUNKS, BLOCK, CHUNK), BF),
            pltpu.VMEM((TILES, BLOCK, BLOCK), BF),
            pltpu.VMEM((D, D), BF),
            pltpu.VMEM((D, D), BF),
            pltpu.VMEM(whole, BF),
            pltpu.VMEM((CELL_DEV, EXT * BLOCK), BF),
            pltpu.VMEM((CELL_DEV, CELL_DEV), BF),
            pltpu.VMEM((EXT * BLOCK, CELL_DEV), BF),
            pltpu.VMEM((D, D), BF),
            pltpu.VMEM((D, D), BF),
            pltpu.VMEM(whole, F32),
            pltpu.VMEM(whole, F32),
            pltpu.VMEM(whole, F32),
            pltpu.VMEM(whole, BF),
            pltpu.VMEM(whole, BF),
            pltpu.VMEM((CHUNKS, nk, CHUNK), BF),
            pltpu.VMEM(whole, BF),
            pltpu.VMEM(whole, BF),
            pltpu.VMEM((CHUNKS, nk, CHUNK), BF),
            pltpu.VMEM((CHUNKS, n_blk, SN_DEV, CHUNK), BF),
            pltpu.VMEM((CHUNKS, 4, BLOCK, CHUNK), BF),
            pltpu.VMEM((CHUNKS, 4, BLOCK, CHUNK), BF),
            pltpu.VMEM(whole, F32),
            pltpu.VMEM(whole, BF),
            pltpu.VMEM(whole, BF),
            pltpu.VMEM(whole, F32),
            pltpu.VMEM(whole, BF),
            pltpu.VMEM((2, CHUNKS, 2, BLOCK, CHUNK), BF),
            sem((CHUNKS,)), sem((5,)), sem((3,)), sem((CHUNKS, 4)), sem((CHUNKS, 4)),
            sem((CHUNKS, n_blk)), sem((CHUNKS, n_blk)), sem((CHUNKS, n_blk)), sem((CHUNKS, n_blk)),
            sem((CHUNKS, 4)), sem((CHUNKS, 4)), sem((2, CHUNKS, 2)), sem((2, CHUNKS, 2)),
        ],
        compiler_params=pltpu.CompilerParams(
            collective_id=0, has_side_effects=True, vmem_limit_bytes=63 * 1024 * 1024
        ),
    )(cells, tile_rows, tile_cols, tile_count, halo_blocks, tile_vals,
      pool_ids.reshape(1, CELL_DEV), w_msg, w_query, cotangent)
    return pl.pallas_call(
        hand_over,
        out_shape=[jax.ShapeDtypeStruct(whole, BF)] * 3,
        in_specs=[any_spec] * 3,
        out_specs=[any_spec] * 3,
        scratch_shapes=[sem((3, 2))],
        compiler_params=pltpu.CompilerParams(vmem_limit_bytes=63 * 1024 * 1024),
    )(*results)


def solution(mesh):
    both = P(("row", "blk"))
    flat = P(("row", "blk"), None)
    return jax.shard_map(
        functools.partial(body, mesh.shape["row"], mesh.shape["blk"]),
        mesh=mesh,
        in_specs=(flat, both, both, both, both, P(("row", "blk"), None, None), both, P(), P(), flat),
        out_specs=(flat, flat, flat),
        check_vma=False,
    )
```

time: 325 us -> 77.6 us (0.24); the launches traced: 320 us -> 77.3 us
  loops' own time: 103 us -> 0 us
  Pallas kernels: 0 us -> 75.3 us
  matrix products: 59.6 us -> 0 us
  local copies, waits for them, and re-layouts: 48 us -> 0 us
  waiting for transfers between devices: 45.6 us -> 0 us
  other arithmetic: 23.6 us -> 0 us
  blocking collectives: 20.8 us -> 0 us
  starting transfers between devices: 17.9 us -> 0 us
    another operation x3 -> x0, loops' own time: 103 us -> none  [the longest x1 52.6 us: body(): lax.fori_loop(0, live_count, add_tile, jnp.zeros((NB, BLOCK, D), jnp.floa...]
    pallas_call x0 -> x2, Pallas kernels: none -> 75.3 us  [the longest x1 38.4 us: body(): pl.pallas_call(functools.partial(kernel, n_row, n_blk), out_shape=[jax.Sh...]
    dot_general x49 -> x0, matrix products: 57.8 us -> none  [the longest x12 21.1 us: back_tile(): lax.dot_general(tile_vals[number], picked, (((0,), (0,)), ((), ())), pref...]
    ppermute x15 -> x0, waiting for transfers between devices: 45.6 us -> none  [the longest x7 26.4 us: from_behind(): lax.ppermute(value, axis, [(i, (i + by) % count) for i in range(count)])]
    dynamic_slice x48 -> x0, local copies, waits for them, and re-layouts: 35.8 us -> none  [the longest x12 14.8 us: add_tile(): tile_cols[number]]
    all_gather x1 -> x0, blocking collectives: 20.8 us -> none  [body(): key_table = lax.all_gather(supern, 'blk', axis=0, tiled=True)]
    ppermute x15 -> x0, starting transfers between devices: 17.9 us -> none  [the longest x4 8.4 us: passed_along(): lax.ppermute(value, axis, [(source, source + steps) for source in range(l...]
    another operation x25 -> x0, other arithmetic: 17.6 us -> none
  transfers between devices with their start and end apart: 15 -> 0, of which waited for: 13 -> 0; matrix products, arithmetic and copies ran while one was open for 5% -> 0% of each run, Pallas kernels for 0% -> 0%
where the time goes in v1:
time: 77.6 us; the launch traced here: 77.3 us
  Pallas kernels  75.3 us (97%)
  between operations  1.93 us (2%)
    pallas_call x1, Pallas kernels, body(): pl.pallas_call(functools.partial(kernel, n_row, n_blk), out_shape=[jax.Sh...  38.4 us
    pallas_call x1, Pallas kernels, body(): pl.pallas_call(hand_over, out_shape=[jax.ShapeDtypeStruct(whole, BF)] * 3...  36.9 us

profile of v1, /device:TPU:0, one launch (start us, length us, event | category | flops | bytes accessed | tf_op | source)
XLA Modules:
  0.0 77.3 jit_solution(10133341631358777676)
XLA Ops:
  1.9 38.4 %shard_map.121 = (bf16[256,768]{1,0:T(8,128)(2,1)}, bf16[256,768]{1,0:T(8,128)(2,1)}, bf16[256,768]{1,0:T(8,128)(2,1)}) custom-call(bf16[256,768]{1,0:T(8,128)(2,1)} %cells.1, s32[12]{0:T(128)} %rows.1, s32[12]{0:T(128)} %colsr.1, s32[1]{0:T(128)S(6)} %copy.13.count, s32[1]{0:T(128)S(6)} %copy.14.halo, bf16[12,128,128]{2,1,0:T(8,128)(2,1)} %tiles.1, ...), custom_call_target="tpu_custom_call" | custom-call | tf_op jit(solution)/shard_map/pallas_call | solution.py:436
  40.4 36.9 %shard_map.122 = (bf16[256,768]{1,0:T(8,128)(2,1)}, bf16[256,768]{1,0:T(8,128)(2,1)}, bf16[256,768]{1,0:T(8,128)(2,1)}) custom-call(bf16[256,768]{1,0:T(8,128)(2,1)} %get-tuple-element.6.a, bf16[256,768]{1,0:T(8,128)(2,1)} %get-tuple-element.7.b, bf16[256,768]{1,0:T(8,128)(2,1)} %get-tuple-element.8.c), custom_call_target="tpu_custom_call" | custom-call | tf_op jit(solution)/shard_map/pallas_call | solution.py:480

commit v2 on v1

--- a/solution.py
+++ b/solution.py
@@ -38,11 +38,11 @@
 
 def kernel(
     n_row, n_blk,
-    cells, rows, colsr, count, halo, tiles, pool, w_msg, w_query, cot,
-    passed_o, att_o, grad_o,
-    ext, bnd, tv, wm, wq, cv, adj, adj_lo, adj_t, wm_t, wq_t, msg, hid, sig, pas, qry, keys,
-    att, dqr, kg, kgr, gs, gr, own, out, dh, base, dm, via,
-    lc, ld, st, hs, hr, ks, kr, ps, pr, ss, sr, vr, vs,
+    cells, rows_h, cols_h, count, halo, tiles, pool_h, w_msg, w_query, cot,
+    pas, att, out,
+    ext, bnd, tv, wm, wq, cv, adj, adj_lo, adj_t, wm_t, wq_t, msg, hid, sig, qry, keys,
+    dqr, kg, kgr, gs, gr, own, dh, base, dm, via, cv_t, sc, sl, pb, ds,
+    lc, ld, hs, hr, ks, kr, ps, pr, ss, sr, vr, vs, rows, colsr, pool, li,
 ):
     r = lax.axis_index("row")
     c = lax.axis_index("blk")
@@ -58,7 +58,12 @@
         pltpu.make_async_copy(cells.at[:, pl.ds(j * CHUNK, CHUNK)], ext.at[j, pl.ds(0, CELL_DEV)], lc.at[j])
         for j in range(CHUNKS)
     ]
-    for load in cell_loads + loads:
+    ints = [
+        pltpu.make_async_copy(rows_h, rows, li.at[0]),
+        pltpu.make_async_copy(cols_h, colsr, li.at[1]),
+        pltpu.make_async_copy(pool_h, pool, li.at[2]),
+    ]
+    for load in cell_loads + ints + loads:
         load.start()
 
     barrier = pltpu.get_barrier_semaphore()
@@ -235,6 +240,8 @@
                 gr[j, s] = jnp.zeros((BLOCK, CHUNK), BF)
 
     loads[0].wait()
+    for load in ints:
+        load.wait()
     live = count[0]
     for i in range(NB):
         at = slice(i * BLOCK, (i + 1) * BLOCK)
@@ -268,6 +275,8 @@
             wm_t[cols(k), cols(j)] = wm[cols(j), cols(k)].T
             wq_t[cols(k), cols(j)] = wq[cols(j), cols(k)].T
     loads[3].wait()
+    for j in range(CHUNKS):
+        cv_t[cols(j), :] = cv[:, cols(j)].T
 
     for j in range(CHUNKS):
         for s in (2, 3):
@@ -291,17 +300,17 @@
             hid[:, cols(k)] = term if j == 0 else hid[:, cols(k)] + term
     mine = pl.ds(pl.multiple_of(c * SN_DEV, SN_DEV), SN_DEV)
     for j in range(CHUNKS):
-        hidden = hid[:, cols(j)] + dot(part, wm[cols(CHUNKS - 1), cols(j)])
-        sigma = jax.nn.sigmoid(hidden)
-        hid[:, cols(j)] = hidden
-        sig[:, cols(j)] = sigma
-        passed = (ext[j, :CELL_DEV].astype(F32) + hidden * sigma).astype(BF)
-        pas[:, cols(j)] = passed
+        hid[:, cols(j)] += dot(part, wm[cols(CHUNKS - 1), cols(j)])
+        for first in range(0, CELL_DEV, 64):
+            some = slice(first, first + 64)
+            hidden = hid[some, cols(j)]
+            sigma = jax.nn.sigmoid(hidden)
+            sig[some, cols(j)] = sigma
+            pas[some, cols(j)] = (ext[j, some].astype(F32) + hidden * sigma).astype(BF)
+        passed = pas[:, cols(j)]
         keys[j, mine] = (dot(member_b, passed) / root).astype(BF)
         for off in range(1, n_blk):
             key_copy(j, off).start()
-    stores = [pltpu.make_async_copy(pas, passed_o, st.at[0])]
-    stores[0].start()
     for j in range(CHUNKS):
         qry[:, cols(j)] = dot(pas[...], wq[:, cols(j)]).astype(BF)
 
@@ -309,6 +318,9 @@
     even_f = (lane < HEAD).astype(F32)
     even, odd = even_f.astype(BF), (1.0 - even_f).astype(BF)
     scale = HEAD ** (-0.5)
+    line = lax.broadcasted_iota(jnp.int32, (PAIR, 1), 0)
+    upper_f = (line < HEAD).astype(F32)
+    upper, lower = upper_f.astype(BF), (1.0 - upper_f).astype(BF)
     per = CHUNK // PAIR
     for t in range(D // PAIR):
         at = cols(t, PAIR)
@@ -318,26 +330,32 @@
                 key_recv(group, off).wait_recv()
         kp = keys[group, :, inner]
         k2 = jnp.concatenate([kp * even, kp * odd], axis=0)
+        kp_t = kp.T
+        k2_t = jnp.concatenate([kp_t * upper, kp_t * lower], axis=1)
         qp, cp = qry[:, at], cv[:, at]
-        scores = dot_nt(k2, qp).reshape(2, nk, CELL_DEV)
-        slope = dot_nt(k2, cp).reshape(2, nk, CELL_DEV)
-        top = jnp.max(scores, axis=1, keepdims=True)
-        probs = jnp.exp2((scores - top) * (scale * LOG2E))
-        probs = probs * (1.0 / jnp.sum(probs, axis=1, keepdims=True))
-        rounded = probs.astype(BF)
-        centre = jnp.sum(rounded.astype(F32) * slope, axis=1, keepdims=True)
-        dscore = (probs * (slope - centre) * scale).astype(BF)
-        rounded = rounded.reshape(2 * nk, CELL_DEV)
-        dscore = dscore.reshape(2 * nk, CELL_DEV)
-        both = dot(dscore, qp) + dot(rounded, cp)
+        w = t % 2
+        sc[w] = dot_nt(k2, qp)
+        sl[w] = dot(k2, cv_t[at, :])
+        for h in range(2):
+            head = slice(h * nk, (h + 1) * nk)
+            for x in range(CELL_DEV // BLOCK):
+                some = cols(x, BLOCK)
+                scores = sc[w, head, some]
+                top = jnp.max(scores, axis=0, keepdims=True)
+                probs = jnp.exp2((scores - top) * (scale * LOG2E))
+                probs = probs * (1.0 / jnp.sum(probs, axis=0, keepdims=True))
+                rounded = probs.astype(BF)
+                pb[w, head, some] = rounded
+                slope = sl[w, head, some]
+                centre = jnp.sum(rounded.astype(F32) * slope, axis=0, keepdims=True)
+                ds[w, head, some] = (probs * (slope - centre) * scale).astype(BF)
+        both = dot(ds[w], qp) + dot(pb[w], cp)
         kg[group, :, inner] = jnp.where(lane < HEAD, both[:nk], both[nk:]).astype(BF)
         if t % per == per - 1:
             for off in range(1, n_blk):
                 part_copy(group, off).start()
-        att[:, at] = dot(rounded.T, k2).astype(BF)
-        dqr[:, at] = dot(dscore.T, k2).astype(BF)
-    stores.append(pltpu.make_async_copy(att, att_o, st.at[1]))
-    stores[1].start()
+        att[:, at] = dot(k2_t, pb[w]).astype(BF).T
+        dqr[:, at] = dot(k2_t, ds[w]).astype(BF).T
     for j in range(CHUNKS):
         base[:, cols(j)] = cv[:, cols(j)].astype(F32) + dot(dqr[...], wq_t[:, cols(j)])
         sigma = sig[:, cols(j)]
@@ -380,8 +398,6 @@
         )
         out[:BLOCK, cols(j)] = (own[:BLOCK, cols(j)] + returned * (1.0 - second)).astype(BF)
         out[BLOCK:, cols(j)] = (own[BLOCK:, cols(j)] + returned * second).astype(BF)
-    stores.append(pltpu.make_async_copy(out, grad_o, st.at[2]))
-    stores[2].start()
 
     for s in range(4):
         @pl.when(straight(s))
@@ -406,8 +422,6 @@
         for j in range(CHUNKS):
             key_copy(j, off).wait_send()
             part_copy(j, off).wait_send()
-    for store in stores:
-        store.wait()
 
 
 def hand_over(a, b, c, a_o, b_o, c_o, sems):
@@ -429,15 +443,15 @@
          w_msg, w_query, cotangent):
     any_spec = pl.BlockSpec(memory_space=pl.ANY)
     smem = pl.BlockSpec(memory_space=pltpu.SMEM)
-    vmem = pl.BlockSpec(memory_space=pltpu.VMEM)
+    hbm = pl.BlockSpec(memory_space=pltpu.HBM)
     nk = SN_DEV * n_blk
     whole = (CELL_DEV, D)
     sem = pltpu.SemaphoreType.DMA
     results = pl.pallas_call(
         functools.partial(kernel, n_row, n_blk),
-        out_shape=[jax.ShapeDtypeStruct(whole, BF)] * 3,
-        in_specs=[any_spec, smem, smem, smem, smem, any_spec, vmem, any_spec, any_spec, any_spec],
-        out_specs=[any_spec] * 3,
+        out_shape=[pltpu.VMEM(whole, BF)] * 3,
+        in_specs=[hbm, hbm, hbm, smem, smem, hbm, hbm, hbm, hbm, hbm],
+        out_specs=[pl.BlockSpec(memory_space=pltpu.VMEM)] * 3,
         scratch_shapes=[
             pltpu.VMEM((CHUNKS, EXT * BLOCK, CHUNK), BF),
             pltpu.VMEM((CHUNKS, BLOCK, CHUNK), BF),
@@ -454,9 +468,7 @@
             pltpu.VMEM(whole, F32),
             pltpu.VMEM(whole, F32),
             pltpu.VMEM(whole, BF),
-            pltpu.VMEM(whole, BF),
             pltpu.VMEM((CHUNKS, nk, CHUNK), BF),
-            pltpu.VMEM(whole, BF),
             pltpu.VMEM(whole, BF),
             pltpu.VMEM((CHUNKS, nk, CHUNK), BF),
             pltpu.VMEM((CHUNKS, n_blk, SN_DEV, CHUNK), BF),
@@ -464,16 +476,22 @@
             pltpu.VMEM((CHUNKS, 4, BLOCK, CHUNK), BF),
             pltpu.VMEM(whole, F32),
             pltpu.VMEM(whole, BF),
-            pltpu.VMEM(whole, BF),
             pltpu.VMEM(whole, F32),
             pltpu.VMEM(whole, BF),
             pltpu.VMEM((2, CHUNKS, 2, BLOCK, CHUNK), BF),
-            sem((CHUNKS,)), sem((5,)), sem((3,)), sem((CHUNKS, 4)), sem((CHUNKS, 4)),
+            pltpu.VMEM((D, CELL_DEV), BF),
+            pltpu.VMEM((2, 2 * nk, CELL_DEV), F32),
+            pltpu.VMEM((2, 2 * nk, CELL_DEV), F32),
+            pltpu.VMEM((2, 2 * nk, CELL_DEV), BF),
+            pltpu.VMEM((2, 2 * nk, CELL_DEV), BF),
+            sem((CHUNKS,)), sem((5,)), sem((CHUNKS, 4)), sem((CHUNKS, 4)),
             sem((CHUNKS, n_blk)), sem((CHUNKS, n_blk)), sem((CHUNKS, n_blk)), sem((CHUNKS, n_blk)),
             sem((CHUNKS, 4)), sem((CHUNKS, 4)), sem((2, CHUNKS, 2)), sem((2, CHUNKS, 2)),
+            pltpu.SMEM((TILES,), jnp.int32), pltpu.SMEM((TILES,), jnp.int32),
+            pltpu.VMEM((1, CELL_DEV), jnp.int32), sem((3,)),
         ],
         compiler_params=pltpu.CompilerParams(
-            collective_id=0, has_side_effects=True, vmem_limit_bytes=63 * 1024 * 1024
+            collective_id=0, has_side_effects=True, vmem_limit_bytes=(62 * 1024 + 768) * 1024
         ),
     )(cells, tile_rows, tile_cols, tile_count, halo_blocks, tile_vals,
       pool_ids.reshape(1, CELL_DEV), w_msg, w_query, cotangent)
@@ -481,9 +499,8 @@
         hand_over,
         out_shape=[jax.ShapeDtypeStruct(whole, BF)] * 3,
         in_specs=[any_spec] * 3,
-        out_specs=[any_spec] * 3,
+        out_specs=[hbm] * 3,
         scratch_shapes=[sem((3, 2))],
-        compiler_params=pltpu.CompilerParams(vmem_limit_bytes=63 * 1024 * 1024),
     )(*results)
 
 

time: 77.6 us -> 79.1 us (1.019)
  local copies, waits for them, and re-layouts: 0 us -> 2.23 us
    unnamed x0 -> x6, local copies, waits for them, and re-layouts: none -> 2.23 us
where the time goes in v2:
time: 79.1 us; the launch traced here: 78.9 us
  Pallas kernels  74.7 us (94%)
  local copies, waits for them, and re-layouts  2.23 us (3%)
  between operations  1.94 us (2%)
    pallas_call x1, Pallas kernels, body(): pl.pallas_call(functools.partial(kernel, n_row, n_blk), out_shape=[pltpu....  37.8 us
    pallas_call x1, Pallas kernels, body(): pl.pallas_call(hand_over, out_shape=[jax.ShapeDtypeStruct(whole, BF)] * 3...  36.9 us
    unnamed x6, local copies, waits for them, and re-layouts  2.23 us

profile of v2, /device:TPU:0, one launch (start us, length us, event | category | flops | bytes accessed | tf_op | source)
XLA Modules:
  0.0 78.9 jit_solution(6272291321782614634)
XLA Ops:
  1.9 37.8 %shard_map.121 = (bf16[256,768]{1,0:T(8,128)(2,1)S(1)}, bf16[256,768]{1,0:T(8,128)(2,1)S(1)}, bf16[256,768]{1,0:T(8,128)(2,1)S(1)}) custom-call(bf16[256,768]{1,0:T(8,128)(2,1)} %cells.1, s32[12]{0:T(128)} %rows_h.1, s32[12]{0:T(128)} %cols_h.1, s32[1]{0:T(128)S(6)} %copy.13.count, s32[1]{0:T(128)S(6)} %copy.14.halo, bf16[12,128,128]{2,1,0:T(8,128)(2,1)} %tiles.1, ...), custom_call_target="tpu_custom_call" | custom-call | tf_op jit(solution)/shard_map/pallas_call | solution.py:450
  39.8 0.0 copy-start
  39.8 0.7 copy-done
  40.5 0.0 copy-start.1
  40.5 0.7 copy-done.1
  41.3 0.0 copy-start.2
  41.3 0.7 copy-done.2
  42.0 36.9 %shard_map.122 = (bf16[256,768]{1,0:T(8,128)(2,1)}, bf16[256,768]{1,0:T(8,128)(2,1)}, bf16[256,768]{1,0:T(8,128)(2,1)}) custom-call(bf16[256,768]{1,0:T(8,128)(2,1)} %copy-done, bf16[256,768]{1,0:T(8,128)(2,1)} %copy-done.1, bf16[256,768]{1,0:T(8,128)(2,1)} %copy-done.2), custom_call_target="tpu_custom_call" | custom-call | tf_op jit(solution)/shard_map/pallas_call | solution.py:498
Async XLA Ops:
  39.8 0.8 copy-start
  40.5 0.7 copy-start.1
  41.3 0.7 copy-start.2

commit v3 on v2

--- a/solution.py
+++ b/solution.py
@@ -256,11 +256,14 @@
         for k in range(NB, EXT):
             use = (rows[k] == i).astype(F32)
             adj[at, k * BLOCK : (k + 1) * BLOCK] = (tv[k].astype(F32) * use).astype(BF)
+    hand_on(0, 0)
     for k in range(CHUNKS):
         adj_t[cols(k), :] = adj[:, cols(k)].T
+    hand_on(0, 1)
     for j in range(CHUNKS):
         own_cells = ext[j, :CELL_DEV]
         msg[:, cols(j)] = dot(adj[:, :CELL_DEV], own_cells) + dot(adj_lo[...], own_cells)
+    hand_on(0, 2)
     ids = pool[...]
     member = (ids == lax.broadcasted_iota(jnp.int32, (SN_DEV, CELL_DEV), 0)).astype(F32)
     member_b = member.astype(BF)
@@ -270,7 +273,6 @@
     loads[1].wait()
     loads[2].wait()
     for j in range(CHUNKS):
-        hand_on(0, j)
         for k in range(CHUNKS):
             wm_t[cols(k), cols(j)] = wm[cols(j), cols(k)].T
             wq_t[cols(k), cols(j)] = wq[cols(j), cols(k)].T
@@ -424,30 +426,14 @@
             part_copy(j, off).wait_send()
 
 
-def hand_over(a, b, c, a_o, b_o, c_o, sems):
-    half = CELL_DEV // 2
-    copies = [
-        pltpu.make_async_copy(
-            source.at[pl.ds(k * half, half)], target.at[pl.ds(k * half, half)], sems.at[i, k]
-        )
-        for i, (source, target) in enumerate(((a, a_o), (b, b_o), (c, c_o)))
-        for k in range(2)
-    ]
-    for copy in copies:
-        copy.start()
-    for copy in copies:
-        copy.wait()
-
-
 def body(n_row, n_blk, cells, tile_rows, tile_cols, tile_count, halo_blocks, tile_vals, pool_ids,
          w_msg, w_query, cotangent):
-    any_spec = pl.BlockSpec(memory_space=pl.ANY)
     smem = pl.BlockSpec(memory_space=pltpu.SMEM)
     hbm = pl.BlockSpec(memory_space=pltpu.HBM)
     nk = SN_DEV * n_blk
     whole = (CELL_DEV, D)
     sem = pltpu.SemaphoreType.DMA
-    results = pl.pallas_call(
+    return pl.pallas_call(
         functools.partial(kernel, n_row, n_blk),
         out_shape=[pltpu.VMEM(whole, BF)] * 3,
         in_specs=[hbm, hbm, hbm, smem, smem, hbm, hbm, hbm, hbm, hbm],
@@ -495,13 +481,6 @@
         ),
     )(cells, tile_rows, tile_cols, tile_count, halo_blocks, tile_vals,
       pool_ids.reshape(1, CELL_DEV), w_msg, w_query, cotangent)
-    return pl.pallas_call(
-        hand_over,
-        out_shape=[jax.ShapeDtypeStruct(whole, BF)] * 3,
-        in_specs=[any_spec] * 3,
-        out_specs=[hbm] * 3,
-        scratch_shapes=[sem((3, 2))],
-    )(*results)
 
 
 def solution(mesh):

time: 79.1 us -> 42.2 us (0.53)
  Pallas kernels: 74.7 us -> 37.9 us
    pallas_call x1 -> x0, Pallas kernels: 36.9 us -> none  [body(): pl.pallas_call(hand_over, out_shape=[jax.ShapeDtypeStruct(whole, BF)] * 3...]
    unnamed x6 -> x3, local copies, waits for them, and re-layouts: 2.23 us -> 2.24 us
where the time goes in v3:
time: 42.2 us; the launch traced here: 42 us
  Pallas kernels  37.9 us (90%)
  local copies, waits for them, and re-layouts  2.24 us (5%)
  between operations  1.93 us (5%)
    pallas_call x1, Pallas kernels, body(): pl.pallas_call(functools.partial(kernel, n_row, n_blk), out_shape=[pltpu....  37.9 us
    unnamed x3, local copies, waits for them, and re-layouts  2.24 us

profile of v3, /device:TPU:0, one launch (start us, length us, event | category | flops | bytes accessed | tf_op | source)
XLA Modules:
  0.0 42.0 jit_solution(5797028303507361415)
XLA Ops:
  1.9 37.9 %shard_map.121 = (bf16[256,768]{1,0:T(8,128)(2,1)S(1)}, bf16[256,768]{1,0:T(8,128)(2,1)S(1)}, bf16[256,768]{1,0:T(8,128)(2,1)S(1)}) custom-call(bf16[256,768]{1,0:T(8,128)(2,1)} %cells.1, s32[12]{0:T(128)} %rows_h.1, s32[12]{0:T(128)} %cols_h.1, s32[1]{0:T(128)S(6)} %copy.19.count, s32[1]{0:T(128)S(6)} %copy.20.halo, bf16[12,128,128]{2,1,0:T(8,128)(2,1)} %tiles.1, ...), custom_call_target="tpu_custom_call" | custom-call | tf_op jit(solution)/shard_map/pallas_call | solution.py:436
  39.8 0.7 %copy.16 = bf16[256,768]{1,0:T(8,128)(2,1)} copy(bf16[256,768]{1,0:T(8,128)(2,1)S(1)} %get-tuple-element.3) | data formatting | bytes 786432
  40.6 0.7 %copy.17 = bf16[256,768]{1,0:T(8,128)(2,1)} copy(bf16[256,768]{1,0:T(8,128)(2,1)S(1)} %get-tuple-element.4) | data formatting | bytes 786432
  41.3 0.7 %copy.18 = bf16[256,768]{1,0:T(8,128)(2,1)} copy(bf16[256,768]{1,0:T(8,128)(2,1)S(1)} %get-tuple-element.5) | data formatting | bytes 786432
